TPU v7x, 32 devices: a whole 2x2x4 slice. The times are simulated.
32 devices in a mesh: hid: 4 (over y, x), wid: 8 (over z, core).
Axes of the slice: x: 2, y: 2, z: 4, core: 2. Of those that a mesh axis runs over, the one named last changes fastest.
Arguments:
- tokens: bfloat16 [512, 16384], P(None, 'wid'), may hold values from -6 to 6
- gate_quant: bfloat16 [16384, 26624], P('wid', 'hid'), may hold values from -0.046875 to 0.046875
- gate_scale: float32 [128, 208], P('wid', 'hid'), may hold values from 0.25 to 4
- up_quant: bfloat16 [16384, 26624], P('wid', 'hid'), may hold values from -0.046875 to 0.046875
- up_scale: float32 [128, 208], P('wid', 'hid'), may hold values from 0.25 to 4
- down_quant: bfloat16 [26624, 16384], P('hid', 'wid'), may hold values from -0.0390625 to 0.0390625
- down_scale: float32 [208, 128], P('hid', 'wid'), may hold values from 0.25 to 4
Outputs:
- mixed: bfloat16 [512, 16384], P(None, 'wid')
All inputs are finite; a program needn't handle non-finite values.
Results may differ from a plain program's by a relative error of at most 0.03.
Values may be sent and summed in bfloat16 or wider, within the bound.
A program may use at most 256 MiB of HBM per device.

v0:
```python
import jax
import jax.numpy as jnp
from jax import lax
from jax.sharding import PartitionSpec as P

BLK = 128


def dequant(quant, scale):
    rows, cols = quant.shape
    blocks = quant.astype(jnp.float32).reshape(rows // BLK, BLK, cols // BLK, BLK)
    return (blocks * scale[:, None, :, None]).reshape(rows, cols).astype(jnp.bfloat16)


def shards(tokens, gate_quant, gate_scale, up_quant, up_scale, down_quant, down_scale):
    gate_w = dequant(gate_quant, gate_scale)
    up_w = dequant(up_quant, up_scale)
    down_w = dequant(down_quant, down_scale)
    gate_part = (
        jnp.dot(tokens, gate_w, preferred_element_type=jnp.float32)
        .astype(jnp.bfloat16)
        .astype(jnp.float32)
    )
    up_part = (
        jnp.dot(tokens, up_w, preferred_element_type=jnp.float32)
        .astype(jnp.bfloat16)
        .astype(jnp.float32)
    )
    gate_share, up_share = (
        lax.psum_scatter(
            gate_part.astype(jnp.bfloat16), "wid", scatter_dimension=1, tiled=True
        ).astype(jnp.float32),
        lax.psum_scatter(
            up_part.astype(jnp.bfloat16), "wid", scatter_dimension=1, tiled=True
        ).astype(jnp.float32),
    )
    hidden_share = (jax.nn.silu(gate_share) * up_share).astype(jnp.bfloat16)
    partial_out = jnp.dot(
        lax.all_gather(hidden_share, "wid", axis=1, tiled=True),
        down_w,
        preferred_element_type=jnp.float32,
    )
    mixed = lax.psum(partial_out.astype(jnp.bfloat16), "hid")
    return mixed


def solution(mesh):
    return jax.shard_map(
        shards,
        mesh=mesh,
        in_specs=(
            P(None, "wid"),
            P("wid", "hid"),
            P("wid", "hid"),
            P("wid", "hid"),
            P("wid", "hid"),
            P("hid", "wid"),
            P("hid", "wid"),
        ),
        out_specs=P(None, "wid"),
        check_vma=False,
    )
```

profile of v0, /device:TPU:0, one launch (start us, length us, event | category | flops | bytes accessed | tf_op | source)
XLA Modules:
  0.0 475.6 jit_solution(17975614082228171537)
XLA Ops:
  6.5 0.0 copy-start
  6.5 0.0 reduce-scatter.3.cloned.1.call-start
  6.5 0.9 copy.10
  7.5 36.3 %copy.9 = bf16[2048,6656]{0,1:T(8,128)(2,1)} copy(bf16[2048,6656]{1,0:T(8,128)(2,1)} %param.8) | data formatting | bytes 54525952 | tf_op args[1]
  43.8 17.4 %mul.40 = f32[16,128,52,128]{1,0,3,2:T(8,128)} broadcast(f32[16,52]{0,1:T(8,128)S(1)} %copy.10), dimensions={0,2} | broadcast | bytes 54529280 | tf_op jit(solution)/shard_map/mul | solution.py:12
  61.2 0.0 copy-done
  61.2 0.0 copy-start.2
  61.2 37.7 %fusion.15 = bf16[512,6656]{0,1:T(8,128)(2,1)} fusion(bf16[512,2048]{1,0:T(8,128)(2,1)S(1)} %copy-done, f32[832,8,16,128]{3,2,1,0:T(8,128)} %bitcast.43, bf16[2048,6656]{0,1:T(8,128)(2,1)} %copy.9), kind=kOutput, calls=%fused_computation.11 | convolution fusion | flops 14002946048 | bytes 90701824 | tf_op jit(solution)/shard_map/dot_general | solution.py:20
  98.9 0.0 reduce-scatter.3.cloned.1.call-update
  99.0 0.2 reduce-scatter.5.cloned.1.call-start
  99.2 0.0 copy-done.2
  99.2 0.1 copy.12
  99.3 36.5 %copy.11 = bf16[2048,6656]{0,1:T(8,128)(2,1)} copy(bf16[2048,6656]{1,0:T(8,128)(2,1)} %param.10) | data formatting | bytes 54525952 | tf_op args[3]
  135.8 17.6 %mul.44 = f32[16,128,52,128]{1,0,3,2:T(8,128)} broadcast(f32[16,52]{0,1:T(8,128)S(1)} %copy.12), dimensions={0,2} | broadcast | bytes 54529280 | tf_op jit(solution)/shard_map/mul | solution.py:12
  153.4 0.0 copy-start.3
  153.4 38.1 %fusion.18 = bf16[512,6656]{0,1:T(8,128)(2,1)} fusion(bf16[512,2048]{1,0:T(8,128)(2,1)S(1)} %copy-done, f32[832,8,16,128]{3,2,1,0:T(8,128)} %bitcast.44, bf16[2048,6656]{0,1:T(8,128)(2,1)} %copy.11), kind=kOutput, calls=%fused_computation.12 | convolution fusion | flops 14002946048 | bytes 90701824 | tf_op jit(solution)/shard_map/dot_general | solution.py:25
  191.5 0.0 reduce-scatter.5.cloned.1.call-update
  191.5 0.0 all-gather.2.cloned.1.call-start
  191.6 0.0 reduce-scatter.3.cloned.1.call-done
  191.6 74.8 %reduce-scatter.5.cloned.1.call-done = bf16[512,832]{0,1:T(8,128)(2,1)} async-done(((bf16[512,6656]{0,1:T(8,128)(2,1)}), bf16[512,832]{0,1:T(8,128)(2,1)}) %reduce-scatter.5.cloned.1.call-update) | async-done | bytes 851984 | tf_op jit(solution)/shard_map/reduce_scatter | solution.py:33
  266.4 2.8 fusion.28
  269.3 0.0 all-gather.2.cloned.1.call-update
  269.3 0.3 all-reduce.2.cloned.1.call-start
  269.6 0.0 copy-done.3
  269.6 0.1 copy.13
  269.7 67.2 %all-gather.2.cloned.1.call-done = bf16[512,6656]{0,1:T(8,128)(2,1)} async-done(((bf16[512,832]{0,1:T(8,128)(2,1)}), bf16[512,6656]{0,1:T(8,128)(2,1)}) %all-gather.2.cloned.1.call-update) | async-done | bytes 6815760 | tf_op jit(solution)/shard_map/all_gather | solution.py:39
  336.9 17.4 %mul.48 = f32[52,128,16,128]{3,2,1,0:T(8,128)} broadcast(f32[52,16]{1,0:T(8,128)S(1)} %copy.13), dimensions={0,2} | broadcast | bytes 54529280 | tf_op jit(solution)/shard_map/mul | solution.py:12
  354.3 0.0 copy-start.1
  354.3 43.2 %fusion.21 = bf16[512,2048]{1,0:T(8,128)(2,1)} fusion(bf16[512,6656]{0,1:T(8,128)(2,1)} %all-gather.2.cloned.1.call-done, f32[832,8,16,128]{3,2,1,0:T(8,128)} %bitcast.42, bf16[6656,2048]{1,0:T(8,128)(2,1)} %param.12), kind=kOutput, calls=%fused_computation.13 | convolution fusion | flops 14000586752 | bytes 90701824 | tf_op jit(solution)/shard_map/dot_general | solution.py:38
  397.5 0.0 all-reduce.2.cloned.1.call-update
  397.5 68.4 %all-reduce.2.cloned.1.call-done = bf16[512,2048]{1,0:T(8,128)(2,1)} async-done(((bf16[512,2048]{1,0:T(8,128)(2,1)}), bf16[512,2048]{1,0:T(8,128)(2,1)}) %all-reduce.2.cloned.1.call-update) | async-done | bytes 2097168 | tf_op jit(solution)/shard_map/psum | solution.py:43
  465.9 3.2 copy.34
  469.1 0.0 copy-done.1
Async XLA Ops:
  6.5 54.7 %copy-start = (bf16[512,2048]{1,0:T(8,128)(2,1)S(1)}, bf16[512,2048]{1,0:T(8,128)(2,1)}, u32[]{:S(2)}) copy-start(bf16[512,2048]{1,0:T(8,128)(2,1)} %param.7) | copy-start | bytes 6291460
  6.5 185.1 %reduce-scatter.3.cloned.1.call-start = ((), (), s32[]{:S(2)}) async-start(), calls=%async_computation.2 | async-start | bytes 7667712 | tf_op jit(solution)/shard_map/reduce_scatter | solution.py:30
  61.2 38.0 %copy-start.2 = (f32[16,52]{1,0:T(8,128)S(1)}, f32[16,52]{1,0:T(8,128)}, u32[]{:S(2)}) copy-start(f32[16,52]{1,0:T(8,128)} %param.11) | copy-start | bytes 9988
  99.0 167.5 %reduce-scatter.5.cloned.1.call-start = ((), (), s32[]{:S(2)}) async-start(), calls=%async_computation.3 | async-start | bytes 7667712 | tf_op jit(solution)/shard_map/reduce_scatter | solution.py:33
  153.4 116.1 %copy-start.3 = (f32[52,16]{0,1:T(8,128)S(1)}, f32[52,16]{0,1:T(8,128)}, u32[]{:S(2)}) copy-start(f32[52,16]{0,1:T(8,128)} %param.13) | copy-start | bytes 9988
  191.5 145.4 %all-gather.2.cloned.1.call-start = ((), (), s32[]{:S(2)}) async-start(), calls=%async_computation.4 | async-start | bytes 7667712 | tf_op jit(solution)/shard_map/all_gather | solution.py:39
  269.3 196.6 %all-reduce.2.cloned.1.call-start = ((), (), s32[]{:S(2)}) async-start(), calls=%async_computation.5 | async-start | bytes 4194304 | tf_op jit(solution)/shard_map/psum | solution.py:43
  354.3 114.8 %copy-start.1 = (bf16[512,2048]{1,0:T(8,128)(2,1)S(1)}, bf16[512,2048]{1,0:T(8,128)(2,1)}, u32[]{:S(2)}) copy-start(bf16[512,2048]{1,0:T(8,128)(2,1)} %param.7) | copy-start | bytes 6291460
Sparse Core Ops, SparseCore 0:
  99.1 77.4 reduce-scatter.2
  191.7 74.7 reduce-scatter.4
  269.4 67.4 all-gather.1
  397.6 68.2 all-reduce.1
where the time goes:
time: 478 us; the launch traced here: 476 us
  waiting for transfers between devices  211 us (44%)
  local copies, waits for them, and re-layouts  130 us (27%)
  matrix products  119 us (25%)
  between operations  13.2 us (3%)
    unnamed x14, local copies, waits for them, and re-layouts  77.2 us
    reduce_scatter x1, waiting for transfers between devices, shards(): lax.psum_scatter(up_part.astype(jnp.bfloat16), 'wid', scatter_dimension=1...  74.8 us
    psum x1, waiting for transfers between devices, shards(): mixed = lax.psum(partial_out.astype(jnp.bfloat16), 'hid')  68.4 us
    all_gather x1, waiting for transfers between devices, shards(): lax.all_gather(hidden_share, 'wid', axis=1, tiled=True)  67.2 us
    mul x3, local copies, waits for them, and re-layouts, dequant(): blocks * scale[:, None, :, None]  52.5 us
    dot_general x1, matrix products, shards(): jnp.dot(lax.all_gather(hidden_share, 'wid', axis=1, tiled=True), down_w,...  43.2 us
    dot_general x1, matrix products, shards(): jnp.dot(tokens, up_w, preferred_element_type=jnp.float32)  38.1 us
    dot_general x1, matrix products, shards(): jnp.dot(tokens, gate_w, preferred_element_type=jnp.float32)  37.7 us
  transfers between devices with their start and end apart: 4, of which 3 were waited for; matrix products, arithmetic and copies ran while one was open for 19% of the time, Pallas kernels for 0%

commit v1 on v0

v1 whole, which is shorter than its diff:
```python
import functools

import jax
import jax.numpy as jnp
from jax import lax
from jax.experimental import pallas as pl
from jax.experimental.pallas import tpu as pltpu
from jax.sharding import PartitionSpec as P

BLK = 128
UNITS = 4 * BLK
GROUPS = 2
LAG_SUM = 1
LAG_HID = 1
MESH = pl.DeviceIdType.MESH


def kernel(
    n_hid, n_wid,
    x_ref, gq_ref, gs_ref, uq_ref, us_ref, dq_ref, ds_ref,
    out_ref,
    part, swap_out, swap_in, chain_in, hid, acc, gbuf, ubuf, dbuf, gu_w, down_w,
    share_out, share_in,
    w_sem, swap_s, swap_r, sum_s, sum_r, hid_s, hid_r, pair_s, pair_r,
    rs_s, rs_r, ag_s, ag_r,
):
    rows, depth = x_ref.shape
    width = out_ref.shape[1]
    chunks = gq_ref.shape[1] // UNITS
    rg = rows // GROUPS
    items = GROUPS * chunks
    chips = n_wid // 2
    slots = swap_out.shape[0]
    own_rows = rg // n_hid

    me_h, me_w = lax.axis_index("hid"), lax.axis_index("wid")
    core, chip = lax.rem(me_w, 2), lax.div(me_w, 2)
    sibling = (me_h, me_w + 1 - 2 * core)
    place = (chips - 1 - chip, chip)
    onward = ((me_h, me_w - 2), (me_h, me_w + 2))
    back = (onward[1], onward[0])

    def hid_peer(k):
        return (lax.rem(me_h + k, n_hid), me_w)

    barrier = pltpu.get_barrier_semaphore()

    def greet(dev):
        pl.semaphore_signal(barrier, inc=1, device_id=dev, device_id_type=MESH)

    greet(sibling)
    for k in range(1, n_hid):
        greet(hid_peer(k))

    @pl.when(chip > 0)
    def _():
        greet(onward[0])

    @pl.when(chip < chips - 1)
    def _():
        greet(onward[1])

    def gu_copies(j):
        cols = pl.ds(pl.multiple_of(j * UNITS, UNITS), UNITS)
        return (
            pltpu.make_async_copy(gq_ref.at[:, cols], gbuf, w_sem.at[0]),
            pltpu.make_async_copy(uq_ref.at[:, cols], ubuf, w_sem.at[1]),
        )

    def d_copy(j):
        units = pl.ds(pl.multiple_of(j * UNITS, UNITS), UNITS)
        return pltpu.make_async_copy(dq_ref.at[units], dbuf, w_sem.at[2])

    def remote(src, dst, send, recv, dev):
        return pltpu.make_async_remote_copy(
            src_ref=src, dst_ref=dst, send_sem=send, recv_sem=recv,
            device_id=dev, device_id_type=MESH,
        )

    def swap_copy(side, j):
        return remote(
            swap_out.at[lax.rem(j, slots), side], swap_in.at[side, j],
            swap_s.at[side, j], swap_r.at[side, j], sibling,
        )

    def split(i):
        g, j = lax.div(i, chunks), lax.rem(i, chunks)
        return j, pl.ds(pl.multiple_of(g * rg, rg), rg)

    def sum_copy(side, i):
        j, rs = split(i)
        return remote(
            part.at[side, j, rs], chain_in.at[side, j, rs],
            sum_s.at[side, i], sum_r.at[side, i], onward[side],
        )

    def hid_copy(side, i):
        j, rs = split(i)
        block = hid.at[j, 2 * side + core, rs]
        return remote(block, block, hid_s.at[side, i], hid_r.at[side, i], back[side])

    def pair_copy(side, i, whose):
        j, rs = split(i)
        block = hid.at[j, 2 * side + whose, rs]
        return remote(block, block, pair_s.at[side, i], pair_r.at[side, i], sibling)

    def rs_copy(g, k):
        to = lax.rem(me_h + k, n_hid)
        src = pl.ds(pl.multiple_of(g * rg + to * own_rows, own_rows), own_rows)
        return remote(
            share_out.at[src], share_in.at[g, k], rs_s.at[g, k], rs_r.at[g, k], hid_peer(k)
        )

    def ag_copy(g, k, owner):
        block = out_ref.at[pl.ds(pl.multiple_of(g * rg + owner * own_rows, own_rows), own_rows)]
        return remote(block, block, ag_s.at[g, k], ag_r.at[g, k], hid_peer(k))

    def project(j):
        for c in gu_copies(j):
            c.wait()

        def scale_rows(k, _):
            rs = pl.ds(pl.multiple_of(k * BLK, BLK), BLK)
            for qt in range(4):
                cs = slice(qt * BLK, (qt + 1) * BLK)
                for m, (buf, sc) in enumerate(((gbuf, gs_ref), (ubuf, us_ref))):
                    w = buf[rs, cs].astype(jnp.float32) * sc[k, j * 4 + qt]
                    gu_w[qt, rs, m * BLK : (m + 1) * BLK] = w.astype(jnp.bfloat16)
            return 0

        lax.fori_loop(0, depth // BLK, scale_rows, 0)

        @pl.when(j + 1 < chunks)
        def _():
            for c in gu_copies(j + 1):
                c.start()

        @pl.when(j >= slots)
        def _():
            for side in range(2):
                swap_copy(side, j - slots).wait_send()

        for side in range(2):
            theirs = jnp.dot(
                x_ref[...], gu_w[2 * side + 1 - core], preferred_element_type=jnp.float32
            )
            swap_out[lax.rem(j, slots), side] = theirs.astype(jnp.bfloat16)
            swap_copy(side, j).start()
        for side in range(2):
            mine = jnp.dot(
                x_ref[...], gu_w[2 * side + core], preferred_element_type=jnp.float32
            )
            part[side, j] = mine.astype(jnp.bfloat16)

    def sum_step(side, i):
        j, rs = split(i)

        @pl.when(i < chunks)
        def _():
            swap_copy(side, j).wait_recv()

        def own():
            return part[side, j, rs].astype(jnp.float32) + swap_in[side, j, rs].astype(jnp.float32)

        @pl.when(place[side] > 0)
        def _():
            sum_copy(side, i).wait_recv()

        @pl.when(place[side] == 0)
        def _():
            part[side, j, rs] = own().astype(jnp.bfloat16)

        @pl.when((place[side] > 0) & (place[side] < chips - 1))
        def _():
            s = own() + chain_in[side, j, rs].astype(jnp.float32)
            part[side, j, rs] = s.astype(jnp.bfloat16)

        @pl.when(place[side] < chips - 1)
        def _():
            sum_copy(side, i).start()

        @pl.when(place[side] == chips - 1)
        def _():
            s = own() + chain_in[side, j, rs].astype(jnp.float32)
            gate, up = s[:, :BLK], s[:, BLK:]
            h = gate / (1.0 + jnp.exp(-gate)) * up
            hid[j, 2 * side + core, rs] = h.astype(jnp.bfloat16)
            hid_copy(side, i).start()
            pair_copy(side, i, core).start()

    def hid_step(side, i):
        hid_copy(side, i).wait_recv()

        @pl.when(place[side] > 0)
        def _():
            hid_copy(side, i).start()

        pair_copy(side, i, core).start()

    def down_step(i):
        j, rs = split(i)
        d_copy(j).wait()

        def scale_rows(k, _):
            ks = pl.ds(pl.multiple_of(k * BLK, BLK), BLK)
            for b in range(width // BLK):
                cs = slice(b * BLK, (b + 1) * BLK)
                w = dbuf[ks, cs].astype(jnp.float32) * ds_ref[j * 4 + k, b]
                down_w[ks, cs] = w.astype(jnp.bfloat16)
            return 0

        lax.fori_loop(0, UNITS // BLK, scale_rows, 0)

        @pl.when(i + 1 < items)
        def _():
            d_copy(lax.rem(i + 1, chunks)).start()

        for side in range(2):
            pair_copy(side, i, 1 - core).wait_recv()
        h = jnp.concatenate([hid[j, qt, rs] for qt in range(4)], axis=1)
        for b in range(width // UNITS):
            cs = slice(b * UNITS, (b + 1) * UNITS)
            acc[rs, cs] += jnp.dot(h, down_w[:, cs], preferred_element_type=jnp.float32)

    def share_send(g):
        rs = slice(g * rg, (g + 1) * rg)
        share_out[rs] = acc[rs].astype(jnp.bfloat16)
        for k in range(1, n_hid):
            rs_copy(g, k).start()

    def share_sum(g):
        block = pl.ds(pl.multiple_of(g * rg + me_h * own_rows, own_rows), own_rows)
        total = share_out[block].astype(jnp.float32)
        for k in range(1, n_hid):
            rs_copy(g, k).wait_recv()
            total = total + share_in[g, k].astype(jnp.float32)
        out_ref[block] = total.astype(jnp.bfloat16)
        for k in range(1, n_hid):
            ag_copy(g, k, me_h).start()

    for c in gu_copies(0):
        c.start()
    d_copy(0).start()
    acc[...] = jnp.zeros_like(acc)
    pl.semaphore_wait(
        barrier,
        n_hid + jnp.where(chip > 0, 1, 0) + jnp.where(chip < chips - 1, 1, 0),
    )

    lag_hid0 = LAG_SUM * (chips - 1)
    lag_down = lag_hid0 + LAG_HID * (chips - 1) + 1
    steps = items + lag_down

    def step(t, _):
        for side in range(2):
            i = t - LAG_SUM * place[side]

            @pl.when((i >= 0) & (i < items))
            def _(side=side, i=i):
                sum_step(side, i)

        for side in range(2):
            hops = chips - 1 - place[side]
            i = t - lag_hid0 - LAG_HID * hops

            @pl.when((hops > 0) & (i >= 0) & (i < items))
            def _(side=side, i=i):
                hid_step(side, i)

        @pl.when(t + 1 < chunks)
        def _():
            project(t + 1)

        i = t - lag_down

        @pl.when(i >= 0)
        def _():
            down_step(i)

        for g in range(GROUPS - 1):
            done = lag_down + (g + 1) * chunks - 1

            @pl.when(t == done)
            def _(g=g):
                share_send(g)

            @pl.when(t == done + min(6, chunks - 1))
            def _(g=g):
                share_sum(g)

        return 0

    lax.fori_loop(-1, steps, step, 0)
    last = GROUPS - 1
    share_send(last)
    share_sum(last)

    for g in range(GROUPS):
        for k in range(1, n_hid):
            ag_copy(g, k, lax.rem(me_h + n_hid - k, n_hid)).wait_recv()
            rs_copy(g, k).wait_send()
            ag_copy(g, k, me_h).wait_send()

    def drain_swap(j, _):
        for side in range(2):
            swap_copy(side, j).wait_send()
        return 0

    lax.fori_loop(max(chunks - slots, 0), chunks, drain_swap, 0)

    def drain(i, _):
        for side in range(2):
            pair_copy(side, i, core).wait_send()

            @pl.when(place[side] < chips - 1)
            def _(side=side):
                sum_copy(side, i).wait_send()

            @pl.when(place[side] > 0)
            def _(side=side):
                hid_copy(side, i).wait_send()

        return 0

    lax.fori_loop(0, items, drain, 0)


def shards(n_hid, n_wid, tokens, gq, gs, uq, us, dq, ds):
    rows, depth = tokens.shape
    units, width = dq.shape
    chunks = units // UNITS
    items = GROUPS * chunks
    rg = rows // GROUPS
    bf16, f32 = jnp.bfloat16, jnp.float32
    dma = pltpu.SemaphoreType.DMA
    whole = pl.BlockSpec(memory_space=pltpu.VMEM)
    hbm = pl.BlockSpec(memory_space=pl.ANY)
    smem = pl.BlockSpec(memory_space=pltpu.SMEM)
    return pl.pallas_call(
        functools.partial(kernel, n_hid, n_wid),
        out_shape=jax.ShapeDtypeStruct((rows, width), bf16),
        in_specs=[whole, hbm, smem, hbm, smem, hbm, smem],
        out_specs=whole,
        scratch_shapes=[
            pltpu.VMEM((2, chunks, rows, 2 * BLK), bf16),
            pltpu.VMEM((2, 2, rows, 2 * BLK), bf16),
            pltpu.VMEM((2, chunks, rows, 2 * BLK), bf16),
            pltpu.VMEM((2, chunks, rows, 2 * BLK), bf16),
            pltpu.VMEM((chunks, 4, rows, BLK), bf16),
            pltpu.VMEM((rows, width), f32),
            pltpu.VMEM((depth, UNITS), bf16),
            pltpu.VMEM((depth, UNITS), bf16),
            pltpu.VMEM((UNITS, width), bf16),
            pltpu.VMEM((4, depth, 2 * BLK), bf16),
            pltpu.VMEM((UNITS, width), bf16),
            pltpu.VMEM((rows, width), bf16),
            pltpu.VMEM((GROUPS, n_hid, rg // n_hid, width), bf16),
            dma((3,)),
            dma((2, chunks)), dma((2, chunks)),
            dma((2, items)), dma((2, items)),
            dma((2, items)), dma((2, items)),
            dma((2, items)), dma((2, items)),
            dma((GROUPS, n_hid)), dma((GROUPS, n_hid)),
            dma((GROUPS, n_hid)), dma((GROUPS, n_hid)),
        ],
        compiler_params=pltpu.CompilerParams(
            collective_id=0, has_side_effects=True, vmem_limit_bytes=60 * 2**20
        ),
        cost_estimate=pl.CostEstimate(
            flops=6 * rows * depth * units,
            bytes_accessed=6 * depth * units,
            transcendentals=rows * units,
        ),
    )(tokens, gq, gs, uq, us, dq, ds)


def solution(mesh):
    return jax.shard_map(
        functools.partial(shards, mesh.shape["hid"], mesh.shape["wid"]),
        mesh=mesh,
        in_specs=(
            P(None, "wid"),
            P("wid", "hid"),
            P("wid", "hid"),
            P("wid", "hid"),
            P("wid", "hid"),
            P("hid", "wid"),
            P("hid", "wid"),
        ),
        out_specs=P(None, "wid"),
        check_vma=False,
    )
```

time: 478 us -> 201 us (0.42)
  waiting for transfers between devices: 211 us -> 0 us
  Pallas kernels: 0 us -> 196 us
  local copies, waits for them, and re-layouts: 130 us -> 4.55 us
  matrix products: 119 us -> 0 us
  between operations: 13.2 us -> 0.01 us
    pallas_call x0 -> x1, Pallas kernels: none -> 196 us  [shards(): pl.pallas_call(functools.partial(kernel, n_hid, n_wid), out_shape=jax.Sha...]
    dot_general x3 -> x0, matrix products: 119 us -> none  [the longest x1 43.2 us: shards(): jnp.dot(lax.all_gather(hidden_share, 'wid', axis=1, tiled=True), down_w,...]
    reduce_scatter x2 -> x0, waiting for transfers between devices: 74.9 us -> none  [the longest x1 74.8 us: shards(): lax.psum_scatter(up_part.astype(jnp.bfloat16), 'wid', scatter_dimension=1...]
    unnamed x14 -> x2, local copies, waits for them, and re-layouts: 77.2 us -> 4.55 us
    psum x1 -> x0, waiting for transfers between devices: 68.4 us -> none  [shards(): mixed = lax.psum(partial_out.astype(jnp.bfloat16), 'hid')]
    all_gather x1 -> x0, waiting for transfers between devices: 67.2 us -> none  [shards(): lax.all_gather(hidden_share, 'wid', axis=1, tiled=True)]
    mul x3 -> x0, local copies, waits for them, and re-layouts: 52.5 us -> none  [dequant(): blocks * scale[:, None, :, None]]
  transfers between devices with their start and end apart: 4 -> 0, of which waited for: 3 -> 0; matrix products, arithmetic and copies ran while one was open for 19% -> 0% of each run, Pallas kernels for 0% -> 0%
where the time goes in v1:
time: 201 us
  Pallas kernels  196 us (98%)
  local copies, waits for them, and re-layouts  4.55 us (2%)
    pallas_call x1, Pallas kernels, shards(): pl.pallas_call(functools.partial(kernel, n_hid, n_wid), out_shape=jax.Sha...  196 us
    unnamed x2, local copies, waits for them, and re-layouts  4.55 us

profile of v1, /device:TPU:0, one launch (start us, length us, event | category | flops | bytes accessed | tf_op | source)
XLA Modules:
  0.0 200.5 jit_solution(4349006719002052021)
XLA Ops:
  0.0 1.4 copy.8.ds_ref
  1.4 196.0 %shard_map.73 = bf16[512,2048]{1,0:T(8,128)(2,1)} custom-call(bf16[512,2048]{1,0:T(8,128)(2,1)} %x_ref.1, bf16[2048,6656]{1,0:T(8,128)(2,1)} %gq_ref.1, f32[16,52]{1,0:T(8,128)} %gs_ref.1, bf16[2048,6656]{1,0:T(8,128)(2,1)} %uq_ref.1, f32[16,52]{1,0:T(8,128)} %us_ref.1, bf16[6656,2048]{1,0:T(8,128)(2,1)} %dq_ref.1, f32[52,16]{1,0:T(8,128)} %copy.8.ds_ref), custom_call_target="tpu_custom_call" | custom-call | flops 41875931136 | bytes 81788928 | tf_op jit(solution)/shard_map/pallas_call | solution.py:339
  197.4 3.2 %copy.10 = bf16[512,2048]{1,0:T(8,128)(2,1)} copy(bf16[512,2048]{1,0:T(8,128)(2,1)} %shard_map.73) | data formatting | bytes 4194304

commit v2 on v1

--- a/solution.py
+++ b/solution.py
@@ -9,9 +9,9 @@
 
 BLK = 128
 UNITS = 4 * BLK
-GROUPS = 2
-LAG_SUM = 1
-LAG_HID = 1
+SUB = 128
+LAG_SUM = 2
+LAG_HID = 2
 MESH = pl.DeviceIdType.MESH
 
 
@@ -20,18 +20,19 @@
     x_ref, gq_ref, gs_ref, uq_ref, us_ref, dq_ref, ds_ref,
     out_ref,
     part, swap_out, swap_in, chain_in, hid, acc, gbuf, ubuf, dbuf, gu_w, down_w,
-    share_out, share_in,
+    share_out, share_in0, share_in1,
     w_sem, swap_s, swap_r, sum_s, sum_r, hid_s, hid_r, pair_s, pair_r,
     rs_s, rs_r, ag_s, ag_r,
 ):
     rows, depth = x_ref.shape
     width = out_ref.shape[1]
     chunks = gq_ref.shape[1] // UNITS
-    rg = rows // GROUPS
-    items = GROUPS * chunks
+    subs = rows // SUB - 1
+    first = subs * chunks
+    items = first + chunks
     chips = n_wid // 2
     slots = swap_out.shape[0]
-    own_rows = rg // n_hid
+    groups = ((0, subs * SUB, share_in0), (subs * SUB, SUB, share_in1))
 
     me_h, me_w = lax.axis_index("hid"), lax.axis_index("wid")
     core, chip = lax.rem(me_w, 2), lax.div(me_w, 2)
@@ -84,8 +85,10 @@
         )
 
     def split(i):
-        g, j = lax.div(i, chunks), lax.rem(i, chunks)
-        return j, pl.ds(pl.multiple_of(g * rg, rg), rg)
+        late = i >= first
+        j = jnp.where(late, i - first, lax.div(i, subs))
+        r = jnp.where(late, subs, lax.rem(i, subs))
+        return j, pl.ds(pl.multiple_of(r * SUB, SUB), SUB)
 
     def sum_copy(side, i):
         j, rs = split(i)
@@ -104,18 +107,23 @@
         block = hid.at[j, 2 * side + whose, rs]
         return remote(block, block, pair_s.at[side, i], pair_r.at[side, i], sibling)
 
+    def owned(g, owner):
+        start, size, _ = groups[g]
+        n = size // n_hid
+        return pl.ds(pl.multiple_of(start + owner * n, n), n)
+
     def rs_copy(g, k):
-        to = lax.rem(me_h + k, n_hid)
-        src = pl.ds(pl.multiple_of(g * rg + to * own_rows, own_rows), own_rows)
-        return remote(
-            share_out.at[src], share_in.at[g, k], rs_s.at[g, k], rs_r.at[g, k], hid_peer(k)
-        )
+        src = share_out.at[owned(g, lax.rem(me_h + k, n_hid))]
+        return remote(src, groups[g][2].at[k], rs_s.at[g, k], rs_r.at[g, k], hid_peer(k))
 
     def ag_copy(g, k, owner):
-        block = out_ref.at[pl.ds(pl.multiple_of(g * rg + owner * own_rows, own_rows), own_rows)]
+        block = out_ref.at[owned(g, owner)]
         return remote(block, block, ag_s.at[g, k], ag_r.at[g, k], hid_peer(k))
 
-    def project(j):
+    def spread(scale):
+        return jnp.full((BLK, BLK), scale, jnp.float32).astype(jnp.bfloat16)
+
+    def scale_gu(j):
         for c in gu_copies(j):
             c.wait()
 
@@ -124,8 +132,7 @@
             for qt in range(4):
                 cs = slice(qt * BLK, (qt + 1) * BLK)
                 for m, (buf, sc) in enumerate(((gbuf, gs_ref), (ubuf, us_ref))):
-                    w = buf[rs, cs].astype(jnp.float32) * sc[k, j * 4 + qt]
-                    gu_w[qt, rs, m * BLK : (m + 1) * BLK] = w.astype(jnp.bfloat16)
+                    gu_w[qt, rs, m * BLK : (m + 1) * BLK] = buf[rs, cs] * spread(sc[k, j * 4 + qt])
             return 0
 
         lax.fori_loop(0, depth // BLK, scale_rows, 0)
@@ -135,27 +142,27 @@
             for c in gu_copies(j + 1):
                 c.start()
 
+    def project_theirs(side, j):
         @pl.when(j >= slots)
         def _():
-            for side in range(2):
-                swap_copy(side, j - slots).wait_send()
-
-        for side in range(2):
-            theirs = jnp.dot(
-                x_ref[...], gu_w[2 * side + 1 - core], preferred_element_type=jnp.float32
-            )
-            swap_out[lax.rem(j, slots), side] = theirs.astype(jnp.bfloat16)
-            swap_copy(side, j).start()
-        for side in range(2):
-            mine = jnp.dot(
-                x_ref[...], gu_w[2 * side + core], preferred_element_type=jnp.float32
-            )
-            part[side, j] = mine.astype(jnp.bfloat16)
+            swap_copy(side, j - slots).wait_send()
+
+        theirs = jnp.dot(
+            x_ref[...], gu_w[2 * side + 1 - core], preferred_element_type=jnp.float32
+        )
+        swap_out[lax.rem(j, slots), side] = theirs.astype(jnp.bfloat16)
+        swap_copy(side, j).start()
+
+    def project_mine(side, j):
+        mine = jnp.dot(
+            x_ref[...], gu_w[2 * side + core], preferred_element_type=jnp.float32
+        )
+        part[side, j] = mine.astype(jnp.bfloat16)
 
     def sum_step(side, i):
         j, rs = split(i)
 
-        @pl.when(i < chunks)
+        @pl.when((i < first) & (lax.rem(i, subs) == 0))
         def _():
             swap_copy(side, j).wait_recv()
 
@@ -197,23 +204,28 @@
 
         pair_copy(side, i, core).start()
 
-    def down_step(i):
-        j, rs = split(i)
+    def scale_down(j, more):
         d_copy(j).wait()
 
         def scale_rows(k, _):
             ks = pl.ds(pl.multiple_of(k * BLK, BLK), BLK)
             for b in range(width // BLK):
                 cs = slice(b * BLK, (b + 1) * BLK)
-                w = dbuf[ks, cs].astype(jnp.float32) * ds_ref[j * 4 + k, b]
-                down_w[ks, cs] = w.astype(jnp.bfloat16)
+                down_w[ks, cs] = dbuf[ks, cs] * spread(ds_ref[j * 4 + k, b])
             return 0
 
         lax.fori_loop(0, UNITS // BLK, scale_rows, 0)
 
-        @pl.when(i + 1 < items)
-        def _():
-            d_copy(lax.rem(i + 1, chunks)).start()
+        @pl.when(more)
+        def _():
+            d_copy(lax.rem(j + 1, chunks)).start()
+
+    def down_step(i):
+        j, rs = split(i)
+
+        @pl.when((i >= first) | (lax.rem(i, subs) == 0))
+        def _():
+            scale_down(j, i + 1 < items)
 
         for side in range(2):
             pair_copy(side, i, 1 - core).wait_recv()
@@ -223,17 +235,18 @@
             acc[rs, cs] += jnp.dot(h, down_w[:, cs], preferred_element_type=jnp.float32)
 
     def share_send(g):
-        rs = slice(g * rg, (g + 1) * rg)
+        start, size, _ = groups[g]
+        rs = slice(start, start + size)
         share_out[rs] = acc[rs].astype(jnp.bfloat16)
         for k in range(1, n_hid):
             rs_copy(g, k).start()
 
     def share_sum(g):
-        block = pl.ds(pl.multiple_of(g * rg + me_h * own_rows, own_rows), own_rows)
+        block = owned(g, me_h)
         total = share_out[block].astype(jnp.float32)
         for k in range(1, n_hid):
             rs_copy(g, k).wait_recv()
-            total = total + share_in[g, k].astype(jnp.float32)
+            total = total + groups[g][2][k].astype(jnp.float32)
         out_ref[block] = total.astype(jnp.bfloat16)
         for k in range(1, n_hid):
             ag_copy(g, k, me_h).start()
@@ -247,6 +260,12 @@
         n_hid + jnp.where(chip > 0, 1, 0) + jnp.where(chip < chips - 1, 1, 0),
     )
 
+    scale_gu(0)
+    for side in range(2):
+        project_theirs(side, 0)
+    for side in range(2):
+        project_mine(side, 0)
+
     lag_hid0 = LAG_SUM * (chips - 1)
     lag_down = lag_hid0 + LAG_HID * (chips - 1) + 1
     steps = items + lag_down
@@ -267,9 +286,21 @@
             def _(side=side, i=i):
                 hid_step(side, i)
 
-        @pl.when(t + 1 < chunks)
-        def _():
-            project(t + 1)
+        j, phase = lax.div(t, subs) + 1, lax.rem(t, subs)
+
+        @pl.when((j < chunks) & (phase == 0))
+        def _():
+            scale_gu(j)
+            project_theirs(0, j)
+
+        @pl.when((j < chunks) & (phase == min(1, subs - 1)))
+        def _():
+            project_theirs(1, j)
+
+        @pl.when((j < chunks) & (phase == subs - 1))
+        def _():
+            project_mine(0, j)
+            project_mine(1, j)
 
         i = t - lag_down
 
@@ -277,25 +308,23 @@
         def _():
             down_step(i)
 
-        for g in range(GROUPS - 1):
-            done = lag_down + (g + 1) * chunks - 1
-
-            @pl.when(t == done)
-            def _(g=g):
-                share_send(g)
-
-            @pl.when(t == done + min(6, chunks - 1))
-            def _(g=g):
-                share_sum(g)
+        done = lag_down + first - 1
+
+        @pl.when(t == done)
+        def _():
+            share_send(0)
+
+        @pl.when(t == done + min(9, chunks - 1))
+        def _():
+            share_sum(0)
 
         return 0
 
-    lax.fori_loop(-1, steps, step, 0)
-    last = GROUPS - 1
-    share_send(last)
-    share_sum(last)
-
-    for g in range(GROUPS):
+    lax.fori_loop(0, steps, step, 0)
+    share_send(1)
+    share_sum(1)
+
+    for g in range(2):
         for k in range(1, n_hid):
             ag_copy(g, k, lax.rem(me_h + n_hid - k, n_hid)).wait_recv()
             rs_copy(g, k).wait_send()
@@ -329,8 +358,7 @@
     rows, depth = tokens.shape
     units, width = dq.shape
     chunks = units // UNITS
-    items = GROUPS * chunks
-    rg = rows // GROUPS
+    items = rows // SUB * chunks
     bf16, f32 = jnp.bfloat16, jnp.float32
     dma = pltpu.SemaphoreType.DMA
     whole = pl.BlockSpec(memory_space=pltpu.VMEM)
@@ -354,14 +382,15 @@
             pltpu.VMEM((4, depth, 2 * BLK), bf16),
             pltpu.VMEM((UNITS, width), bf16),
             pltpu.VMEM((rows, width), bf16),
-            pltpu.VMEM((GROUPS, n_hid, rg // n_hid, width), bf16),
+            pltpu.VMEM((n_hid, (rows - SUB) // n_hid, width), bf16),
+            pltpu.VMEM((n_hid, SUB // n_hid, width), bf16),
             dma((3,)),
             dma((2, chunks)), dma((2, chunks)),
             dma((2, items)), dma((2, items)),
             dma((2, items)), dma((2, items)),
             dma((2, items)), dma((2, items)),
-            dma((GROUPS, n_hid)), dma((GROUPS, n_hid)),
-            dma((GROUPS, n_hid)), dma((GROUPS, n_hid)),
+            dma((2, n_hid)), dma((2, n_hid)),
+            dma((2, n_hid)), dma((2, n_hid)),
         ],
         compiler_params=pltpu.CompilerParams(
             collective_id=0, has_side_effects=True, vmem_limit_bytes=60 * 2**20

time: 201 us -> 182 us (0.905)
  Pallas kernels: 196 us -> 177 us
    pallas_call x1, Pallas kernels: 196 us -> 177 us  [shards(): pl.pallas_call(functools.partial(kernel, n_hid, n_wid), out_shape=jax.Sha...]
where the time goes in v2:
time: 182 us
  Pallas kernels  177 us (97%)
  local copies, waits for them, and re-layouts  4.55 us (2%)
    pallas_call x1, Pallas kernels, shards(): pl.pallas_call(functools.partial(kernel, n_hid, n_wid), out_shape=jax.Sha...  177 us
    unnamed x2, local copies, waits for them, and re-layouts  4.55 us

profile of v2, /device:TPU:0, one launch (start us, length us, event | category | flops | bytes accessed | tf_op | source)
XLA Modules:
  0.0 181.6 jit_solution(11248148501662046952)
XLA Ops:
  0.0 1.4 copy.8.ds_ref
  1.4 177.0 %shard_map.73 = bf16[512,2048]{1,0:T(8,128)(2,1)} custom-call(bf16[512,2048]{1,0:T(8,128)(2,1)} %x_ref.1, bf16[2048,6656]{1,0:T(8,128)(2,1)} %gq_ref.1, f32[16,52]{1,0:T(8,128)} %gs_ref.1, bf16[2048,6656]{1,0:T(8,128)(2,1)} %uq_ref.1, f32[16,52]{1,0:T(8,128)} %us_ref.1, bf16[6656,2048]{1,0:T(8,128)(2,1)} %dq_ref.1, f32[52,16]{1,0:T(8,128)} %copy.8.ds_ref), custom_call_target="tpu_custom_call" | custom-call | flops 41875931136 | bytes 81788928 | tf_op jit(solution)/shard_map/pallas_call | solution.py:367
  178.4 3.2 %copy.10 = bf16[512,2048]{1,0:T(8,128)(2,1)} copy(bf16[512,2048]{1,0:T(8,128)(2,1)} %shard_map.73) | data formatting | bytes 4194304

commit v3 on v2

--- a/solution.py
+++ b/solution.py
@@ -19,7 +19,7 @@
     n_hid, n_wid,
     x_ref, gq_ref, gs_ref, uq_ref, us_ref, dq_ref, ds_ref,
     out_ref,
-    part, swap_out, swap_in, chain_in, hid, acc, gbuf, ubuf, dbuf, gu_w, down_w,
+    part, swap_out, swap_in, chain_in, hid, acc, gbuf, ubuf, dbuf,
     share_out, share_in0, share_in1,
     w_sem, swap_s, swap_r, sum_s, sum_r, hid_s, hid_r, pair_s, pair_r,
     rs_s, rs_r, ag_s, ag_r,
@@ -63,14 +63,16 @@
 
     def gu_copies(j):
         cols = pl.ds(pl.multiple_of(j * UNITS, UNITS), UNITS)
+        slot = lax.rem(j, 2)
         return (
-            pltpu.make_async_copy(gq_ref.at[:, cols], gbuf, w_sem.at[0]),
-            pltpu.make_async_copy(uq_ref.at[:, cols], ubuf, w_sem.at[1]),
+            pltpu.make_async_copy(gq_ref.at[:, cols], gbuf.at[slot], w_sem.at[0, slot]),
+            pltpu.make_async_copy(uq_ref.at[:, cols], ubuf.at[slot], w_sem.at[1, slot]),
         )
 
-    def d_copy(j):
-        units = pl.ds(pl.multiple_of(j * UNITS, UNITS), UNITS)
-        return pltpu.make_async_copy(dq_ref.at[units], dbuf, w_sem.at[2])
+    def d_copy(n):
+        units = pl.ds(pl.multiple_of(lax.rem(n, chunks) * UNITS, UNITS), UNITS)
+        slot = lax.rem(n, 2)
+        return pltpu.make_async_copy(dq_ref.at[units], dbuf.at[slot], w_sem.at[2, slot])
 
     def remote(src, dst, send, recv, dev):
         return pltpu.make_async_remote_copy(
@@ -123,41 +125,39 @@
     def spread(scale):
         return jnp.full((BLK, BLK), scale, jnp.float32).astype(jnp.bfloat16)
 
-    def scale_gu(j):
+    def load_gu(j):
         for c in gu_copies(j):
             c.wait()
 
-        def scale_rows(k, _):
-            rs = pl.ds(pl.multiple_of(k * BLK, BLK), BLK)
-            for qt in range(4):
-                cs = slice(qt * BLK, (qt + 1) * BLK)
-                for m, (buf, sc) in enumerate(((gbuf, gs_ref), (ubuf, us_ref))):
-                    gu_w[qt, rs, m * BLK : (m + 1) * BLK] = buf[rs, cs] * spread(sc[k, j * 4 + qt])
-            return 0
-
-        lax.fori_loop(0, depth // BLK, scale_rows, 0)
-
         @pl.when(j + 1 < chunks)
         def _():
             for c in gu_copies(j + 1):
                 c.start()
 
+    def project(qt, j):
+        slot = lax.rem(j, 2)
+        cols = pl.ds(pl.multiple_of(qt * BLK, BLK), BLK)
+        halves = []
+        for buf, sc in ((gbuf, gs_ref), (ubuf, us_ref)):
+            blocks = [
+                buf[slot, k * BLK : (k + 1) * BLK, cols] * spread(sc[k, j * 4 + qt])
+                for k in range(depth // BLK)
+            ]
+            halves.append(jnp.concatenate(blocks, axis=0))
+        w = jnp.concatenate(halves, axis=1)
+        both = jnp.dot(x_ref[...], w, preferred_element_type=jnp.float32)
+        return both.astype(jnp.bfloat16)
+
     def project_theirs(side, j):
         @pl.when(j >= slots)
         def _():
             swap_copy(side, j - slots).wait_send()
 
-        theirs = jnp.dot(
-            x_ref[...], gu_w[2 * side + 1 - core], preferred_element_type=jnp.float32
-        )
-        swap_out[lax.rem(j, slots), side] = theirs.astype(jnp.bfloat16)
+        swap_out[lax.rem(j, slots), side] = project(2 * side + 1 - core, j)
         swap_copy(side, j).start()
 
     def project_mine(side, j):
-        mine = jnp.dot(
-            x_ref[...], gu_w[2 * side + core], preferred_element_type=jnp.float32
-        )
-        part[side, j] = mine.astype(jnp.bfloat16)
+        part[side, j] = project(2 * side + core, j)
 
     def sum_step(side, i):
         j, rs = split(i)
@@ -204,35 +204,39 @@
 
         pair_copy(side, i, core).start()
 
-    def scale_down(j, more):
-        d_copy(j).wait()
-
-        def scale_rows(k, _):
-            ks = pl.ds(pl.multiple_of(k * BLK, BLK), BLK)
-            for b in range(width // BLK):
-                cs = slice(b * BLK, (b + 1) * BLK)
-                down_w[ks, cs] = dbuf[ks, cs] * spread(ds_ref[j * 4 + k, b])
-            return 0
-
-        lax.fori_loop(0, UNITS // BLK, scale_rows, 0)
-
-        @pl.when(more)
-        def _():
-            d_copy(lax.rem(j + 1, chunks)).start()
-
     def down_step(i):
         j, rs = split(i)
+        n = jnp.where(i >= first, chunks, 0) + j
+        slot = lax.rem(n, 2)
 
         @pl.when((i >= first) | (lax.rem(i, subs) == 0))
         def _():
-            scale_down(j, i + 1 < items)
+            d_copy(n).wait()
+
+            @pl.when(n + 1 < 2 * chunks)
+            def _():
+                d_copy(n + 1).start()
 
         for side in range(2):
             pair_copy(side, i, 1 - core).wait_recv()
         h = jnp.concatenate([hid[j, qt, rs] for qt in range(4)], axis=1)
         for b in range(width // UNITS):
             cs = slice(b * UNITS, (b + 1) * UNITS)
-            acc[rs, cs] += jnp.dot(h, down_w[:, cs], preferred_element_type=jnp.float32)
+            w = jnp.concatenate(
+                [
+                    jnp.concatenate(
+                        [
+                            dbuf[slot, k * BLK : (k + 1) * BLK, m * BLK : (m + 1) * BLK]
+                            * spread(ds_ref[j * 4 + k, m])
+                            for m in range(b * 4, b * 4 + 4)
+                        ],
+                        axis=1,
+                    )
+                    for k in range(4)
+                ],
+                axis=0,
+            )
+            acc[rs, cs] += jnp.dot(h, w, preferred_element_type=jnp.float32)
 
     def share_send(g):
         start, size, _ = groups[g]
@@ -260,7 +264,7 @@
         n_hid + jnp.where(chip > 0, 1, 0) + jnp.where(chip < chips - 1, 1, 0),
     )
 
-    scale_gu(0)
+    load_gu(0)
     for side in range(2):
         project_theirs(side, 0)
     for side in range(2):
@@ -290,7 +294,7 @@
 
         @pl.when((j < chunks) & (phase == 0))
         def _():
-            scale_gu(j)
+            load_gu(j)
             project_theirs(0, j)
 
         @pl.when((j < chunks) & (phase == min(1, subs - 1)))
@@ -376,15 +380,13 @@
             pltpu.VMEM((2, chunks, rows, 2 * BLK), bf16),
             pltpu.VMEM((chunks, 4, rows, BLK), bf16),
             pltpu.VMEM((rows, width), f32),
-            pltpu.VMEM((depth, UNITS), bf16),
-            pltpu.VMEM((depth, UNITS), bf16),
-            pltpu.VMEM((UNITS, width), bf16),
-            pltpu.VMEM((4, depth, 2 * BLK), bf16),
-            pltpu.VMEM((UNITS, width), bf16),
+            pltpu.VMEM((2, depth, UNITS), bf16),
+            pltpu.VMEM((2, depth, UNITS), bf16),
+            pltpu.VMEM((2, UNITS, width), bf16),
             pltpu.VMEM((rows, width), bf16),
             pltpu.VMEM((n_hid, (rows - SUB) // n_hid, width), bf16),
             pltpu.VMEM((n_hid, SUB // n_hid, width), bf16),
-            dma((3,)),
+            dma((3, 2)),
             dma((2, chunks)), dma((2, chunks)),
             dma((2, items)), dma((2, items)),
             dma((2, items)), dma((2, items)),

time: 182 us -> 180 us (0.989)
  Pallas kernels: 177 us -> 175 us
where the time goes in v3:
time: 180 us
  Pallas kernels  175 us (97%)
  local copies, waits for them, and re-layouts  4.55 us (3%)
    pallas_call x1, Pallas kernels, shards(): pl.pallas_call(functools.partial(kernel, n_hid, n_wid), out_shape=jax.Sha...  175 us
    unnamed x2, local copies, waits for them, and re-layouts  4.55 us

profile of v3, /device:TPU:0, one launch (start us, length us, event | category | flops | bytes accessed | tf_op | source)
XLA Modules:
  0.0 179.9 jit_solution(13930874367853070651)
XLA Ops:
  0.0 1.4 copy.8.ds_ref
  1.4 175.4 %shard_map.73 = bf16[512,2048]{1,0:T(8,128)(2,1)} custom-call(bf16[512,2048]{1,0:T(8,128)(2,1)} %x_ref.1, bf16[2048,6656]{1,0:T(8,128)(2,1)} %gq_ref.1, f32[16,52]{1,0:T(8,128)} %gs_ref.1, bf16[2048,6656]{1,0:T(8,128)(2,1)} %uq_ref.1, f32[16,52]{1,0:T(8,128)} %us_ref.1, bf16[6656,2048]{1,0:T(8,128)(2,1)} %dq_ref.1, f32[52,16]{1,0:T(8,128)} %copy.8.ds_ref), custom_call_target="tpu_custom_call" | custom-call | flops 41875931136 | bytes 81788928 | tf_op jit(solution)/shard_map/pallas_call | solution.py:371
  176.8 3.2 %copy.10 = bf16[512,2048]{1,0:T(8,128)(2,1)} copy(bf16[512,2048]{1,0:T(8,128)(2,1)} %shard_map.73) | data formatting | bytes 4194304
